TPU v7x, 32 devices: a whole 2x2x4 slice. The times are simulated.
32 devices in a mesh: fsdp: 8 (over z, x), ctx: 2 (over y), tp: 2 (over core).
Axes of the slice: x: 2, y: 2, z: 4, core: 2. Of those that a mesh axis runs over, the one named last changes fastest.
Arguments:
- tokens: bfloat16 [8, 1024, 896], P('fsdp', 'ctx'), may hold values from -6 to 6
- positions: int32 [8, 1024], P('fsdp', 'ctx'), may hold values from 0 to 1021, as said below
- norm1_gain: bfloat16 [896], P('fsdp'), may hold values from 0.5 to 1.5
- q_weight: bfloat16 [896, 896], P('fsdp', 'tp'), may hold values from -0.1875 to 0.1875
- q_bias: bfloat16 [14, 64], P('tp', 'fsdp'), may hold values from -3 to 3
- key_projection: bfloat16 [896, 128], P('fsdp', 'tp'), may hold values from -0.1875 to 0.1875
- key_bias: bfloat16 [2, 64], P('tp', 'fsdp'), may hold values from -3 to 3
- value_projection: bfloat16 [896, 128], P('fsdp', 'tp'), may hold values from -0.1875 to 0.1875
- value_bias: bfloat16 [2, 64], P('tp', 'fsdp'), may hold values from -3 to 3
- o_weight: bfloat16 [896, 896], P('tp', 'fsdp'), may hold values from -1 to 1
- norm2_gain: bfloat16 [896], P('fsdp'), may hold values from 0.5 to 1.5
- gate_weight: bfloat16 [896, 4864], P('fsdp', 'tp'), may hold values from -0.1875 to 0.1875
- up_weight: bfloat16 [896, 4864], P('fsdp', 'tp'), may hold values from -0.1875 to 0.1875
- down_weight: bfloat16 [4864, 896], P('tp', 'fsdp'), may hold values from -0.25 to 0.25
- out_grad: bfloat16 [8, 1024, 896], P('fsdp', 'ctx'), may hold values from -6 to 6
Outputs:
- layer_out: bfloat16 [8, 1024, 896], P('fsdp', 'ctx')
- input_grad: float32 [8, 1024, 896], P('fsdp', 'ctx')
- norm1_gain_grad: float32 [896], P('fsdp')
- q_weight_grad: float32 [896, 896], P('fsdp', 'tp')
- q_bias_grad: float32 [14, 64], P('tp', 'fsdp')
- k_weight_grad: float32 [896, 128], P('fsdp', 'tp')
- k_bias_grad: float32 [2, 64], P('tp', 'fsdp')
- v_weight_grad: float32 [896, 128], P('fsdp', 'tp')
- v_bias_grad: float32 [2, 64], P('tp', 'fsdp')
- o_weight_grad: float32 [896, 896], P('tp', 'fsdp')
- norm2_gain_grad: float32 [896], P('fsdp')
- gate_weight_grad: float32 [896, 4864], P('fsdp', 'tp')
- up_weight_grad: float32 [896, 4864], P('fsdp', 'tp')
- down_weight_grad: float32 [4864, 896], P('tp', 'fsdp')
Inputs may be any that keep to these rules, and one draw needn't show every extreme that they name: positions count 0, 1, 2, ... along each document and restart at 0 where a new document begins; every sequence begins with a 0.
All inputs are finite; a program needn't handle non-finite values.
Results may differ from a plain program's by a relative error of at most 0.039.
Values may be sent and summed in bfloat16 or wider, within the bound.
No kernel may reach another device: no remote copies, remote signals or barrier semaphores. Data moves between devices by JAX's collectives and lax.ppermute only.
A program may use at most 128 MiB of HBM per device.

v0:
```python
import jax
import jax.numpy as jnp
from jax import lax
from jax.sharding import PartitionSpec as P

NORM_EPS = 1e-06
MASK_FILL = -1e30


def product(left, right):
    return jnp.dot(left, right, preferred_element_type=jnp.float32)


def inner_prod(left, right):
    return lax.dot_general(
        left, right, (((0,), (0,)), ((), ())), preferred_element_type=jnp.float32
    )


def times_trans(left, right):
    return lax.dot_general(
        left, right, (((1,), (1,)), ((), ())), preferred_element_type=jnp.float32
    )


def rotary_apply(tensor, cosine_table, sine_table):
    half_dim = tensor.shape[-1] // 2
    turned = jnp.concatenate([-tensor[..., half_dim:], tensor[..., :half_dim]], axis=-1)
    return tensor * cosine_table + turned * sine_table


def unrotate(upstream, cosine_table, sine_table):
    half_dim = upstream.shape[-1] // 2
    shifted = upstream * sine_table
    turned_back = jnp.concatenate([shifted[..., half_dim:], -shifted[..., :half_dim]], axis=-1)
    return upstream * cosine_table + turned_back


def norm_back(upstream, source, inverse, gain_vec):
    scaled = upstream * gain_vec
    gain_grad = jnp.sum(upstream * source * inverse, axis=0)
    input_part = inverse * scaled - source * inverse**3 * jnp.mean(
        scaled * source, axis=-1, keepdims=True
    )
    return (input_part, gain_grad)


def body(
    tokens,
    positions,
    norm1_gain,
    q_weight,
    q_bias,
    key_projection,
    key_bias,
    value_projection,
    value_bias,
    o_weight,
    norm2_gain,
    gate_weight,
    up_weight,
    down_weight,
    out_grad,
):
    row_count = tokens.shape[1]
    head_dim = key_projection.shape[1]
    head_count = q_weight.shape[1] // head_dim
    query_rows = row_count * head_count
    score_scale = head_dim ** (-0.5)
    gain_one, w_query, b_query, w_key, b_key, value_weight_matrix, value_bias_vector, w_out = (
        lax.all_gather(norm1_gain, "fsdp", axis=0, tiled=True),
        lax.all_gather(q_weight, "fsdp", axis=0, tiled=True),
        lax.all_gather(q_bias, "fsdp", axis=1, tiled=True),
        lax.all_gather(key_projection, "fsdp", axis=0, tiled=True),
        lax.all_gather(key_bias, "fsdp", axis=1, tiled=True),
        lax.all_gather(value_projection, "fsdp", axis=0, tiled=True),
        lax.all_gather(value_bias, "fsdp", axis=1, tiled=True),
        lax.all_gather(o_weight, "fsdp", axis=1, tiled=True),
    )
    gain_two, w_gate, w_up, w_down = (
        lax.all_gather(norm2_gain, "fsdp", axis=0, tiled=True),
        lax.all_gather(gate_weight, "fsdp", axis=0, tiled=True),
        lax.all_gather(up_weight, "fsdp", axis=0, tiled=True),
        lax.all_gather(down_weight, "fsdp", axis=1, tiled=True),
    )
    first_row = lax.axis_index("ctx") * row_count
    seq_total = row_count * lax.axis_size("ctx")
    last_row = first_row + row_count - 1
    inputs = tokens[0].astype(jnp.float32)
    seq_positions = positions[0]
    token_index = first_row + jnp.arange(row_count, dtype=jnp.int32)
    doc_start = token_index - seq_positions
    query_index = jnp.repeat(token_index, head_count)
    query_begin = jnp.repeat(doc_start, head_count)
    inv_freq = 1000000.0 ** (-jnp.arange(0, head_dim, 2, dtype=jnp.float32) / head_dim)
    angles = seq_positions.astype(jnp.float32)[:, None] * inv_freq[None, :]
    angles = jnp.concatenate([angles, angles], axis=-1)
    cosine_table = jnp.cos(angles)
    sine_table = jnp.sin(angles)
    inv_one = lax.rsqrt(jnp.mean(inputs * inputs, axis=-1, keepdims=True) + NORM_EPS)
    first_norm = (inputs * inv_one * gain_one.astype(jnp.float32)).astype(jnp.bfloat16)
    q_lin = product(first_norm, w_query) + b_query.reshape(-1).astype(jnp.float32)
    key_linear = product(first_norm, w_key) + b_key.reshape(-1).astype(jnp.float32)
    value_matrix = (
        product(first_norm, value_weight_matrix) + value_bias_vector.reshape(-1).astype(jnp.float32)
    ).astype(jnp.bfloat16)
    query_matrix = (
        rotary_apply(
            q_lin.reshape(row_count, head_count, head_dim),
            cosine_table[:, None, :],
            sine_table[:, None, :],
        )
        .astype(jnp.bfloat16)
        .reshape(query_rows, head_dim)
    )
    key_row_block = rotary_apply(key_linear, cosine_table, sine_table).astype(jnp.bfloat16)
    key_value = jnp.concatenate([key_row_block, value_matrix], axis=1)

    def visible_at(count):
        key_index = jnp.arange(count, dtype=jnp.int32)
        return (key_index[None, :] <= query_index[:, None]) & (
            key_index[None, :] >= query_begin[:, None]
        )

    start_state = (
        jnp.full((query_rows,), MASK_FILL, jnp.float32),
        jnp.zeros((query_rows,), jnp.float32),
        jnp.zeros((query_rows, head_dim), jnp.float32),
    )
    kv_block = lax.all_gather(key_value, "ctx", axis=0, tiled=True)

    def compute(current):
        top_score, weight_sum, partial_value = current
        key_part = kv_block[:, :head_dim]
        value_part = kv_block[:, head_dim:]
        visible = visible_at(kv_block.shape[0])
        scores = times_trans(query_matrix, key_part) * score_scale
        masked = jnp.where(visible, scores, MASK_FILL)
        new_top = jnp.maximum(top_score, jnp.max(masked, axis=1))
        weights = jnp.where(visible, jnp.exp(scores - new_top[:, None]), 0.0)
        weight_sum = jnp.sum(weights, axis=1)
        partial_value = product(weights.astype(jnp.bfloat16), value_part)
        return (new_top, weight_sum, partial_value)

    top_score, weight_sum, partial_value = lax.cond(
        jnp.int32(0) > last_row, lambda current: current, compute, start_state
    )
    log_total = top_score + jnp.log(weight_sum)
    attn_full = partial_value / weight_sum[:, None]
    attn_low = attn_full.astype(jnp.bfloat16).reshape(row_count, head_count * head_dim)
    middle = inputs + lax.psum(product(attn_low, w_out).astype(jnp.bfloat16), "tp").astype(
        jnp.float32
    )
    inv_two = lax.rsqrt(jnp.mean(middle * middle, axis=-1, keepdims=True) + NORM_EPS)
    norm_two = (middle * inv_two * gain_two.astype(jnp.float32)).astype(jnp.bfloat16)
    gate_proj = product(norm_two, w_gate)
    up_proj = product(norm_two, w_up)
    sigmoid_gate = jax.nn.sigmoid(gate_proj)
    silu_gate = gate_proj * sigmoid_gate
    hidden = (silu_gate * up_proj).astype(jnp.bfloat16)
    layer_out = (
        middle + lax.psum(product(hidden, w_down).astype(jnp.bfloat16), "tp").astype(jnp.float32)
    ).astype(jnp.bfloat16)
    back_set = (
        lax.all_gather(norm1_gain, "fsdp", axis=0, tiled=True),
        lax.all_gather(q_weight, "fsdp", axis=0, tiled=True),
        lax.all_gather(key_projection, "fsdp", axis=0, tiled=True),
        lax.all_gather(value_projection, "fsdp", axis=0, tiled=True),
        lax.all_gather(o_weight, "fsdp", axis=1, tiled=True),
        lax.all_gather(norm2_gain, "fsdp", axis=0, tiled=True),
        lax.all_gather(gate_weight, "fsdp", axis=0, tiled=True),
        lax.all_gather(up_weight, "fsdp", axis=0, tiled=True),
        lax.all_gather(down_weight, "fsdp", axis=1, tiled=True),
    )
    gain_one, w_query, w_key, value_weight_matrix, w_out, gain_two, w_gate, w_up, w_down = back_set
    grad_top = out_grad[0].astype(jnp.float32)
    grad_low = grad_top.astype(jnp.bfloat16)
    down_grad = inner_prod(hidden, grad_low)
    hidden_grad = times_trans(grad_low, w_down)
    gate_grad = (
        hidden_grad * up_proj * sigmoid_gate * (1.0 + gate_proj * (1.0 - sigmoid_gate))
    ).astype(jnp.bfloat16)
    up_grad = (hidden_grad * silu_gate).astype(jnp.bfloat16)
    gate_w_grad = inner_prod(norm_two, gate_grad)
    up_w_grad = inner_prod(norm_two, up_grad)
    norm_two_grad = lax.psum(
        (times_trans(gate_grad, w_gate) + times_trans(up_grad, w_up)).astype(jnp.bfloat16), "tp"
    ).astype(jnp.float32)
    middle_part, gain_two_grad = norm_back(
        norm_two_grad, middle, inv_two, gain_two.astype(jnp.float32)
    )
    middle_grad = grad_top + middle_part
    middle_low = middle_grad.astype(jnp.bfloat16)
    out_w_grad = inner_prod(attn_low, middle_low)
    attn_grad = times_trans(middle_low, w_out).astype(jnp.bfloat16).reshape(query_rows, head_dim)
    row_delta = jnp.sum(attn_grad.astype(jnp.float32) * attn_full, axis=1)
    back_state = (
        jnp.zeros((query_rows, head_dim), jnp.float32),
        jnp.zeros((seq_total, 2 * head_dim), jnp.float32),
    )
    attend_kv_block = lax.all_gather(key_value, "ctx", axis=0, tiled=True)

    def compute(current):
        rows_per_block = attend_kv_block.shape[0]
        key_part = attend_kv_block[:, :head_dim]
        value_part = attend_kv_block[:, head_dim:]
        visible = visible_at(rows_per_block)
        scores = times_trans(query_matrix, key_part) * score_scale
        probabilities = jnp.where(visible, jnp.exp(scores - log_total[:, None]), 0.0)
        prob_grad = times_trans(attn_grad, value_part)
        score_grad = (probabilities * (prob_grad - row_delta[:, None]) * score_scale).astype(
            jnp.bfloat16
        )
        query_acc = product(score_grad, key_part)
        key_part_grad = inner_prod(score_grad, query_matrix)
        value_part_grad = inner_prod(probabilities.astype(jnp.bfloat16), attn_grad)
        update = jnp.concatenate([key_part_grad, value_part_grad], axis=1)
        return (query_acc, update)

    query_acc, pair_grad = lax.cond(
        jnp.int32(0) > last_row, lambda current: current, compute, back_state
    )
    pair_mine = lax.psum_scatter(
        pair_grad.astype(jnp.bfloat16), "ctx", scatter_dimension=0, tiled=True
    ).astype(jnp.float32)
    key_grad = unrotate(pair_mine[:, :head_dim], cosine_table, sine_table).astype(jnp.bfloat16)
    value_grad = pair_mine[:, head_dim:].astype(jnp.bfloat16)
    query_grad = (
        unrotate(
            query_acc.reshape(row_count, head_count, head_dim),
            cosine_table[:, None, :],
            sine_table[:, None, :],
        )
        .astype(jnp.bfloat16)
        .reshape(row_count, head_count * head_dim)
    )
    query_b_grad = jnp.sum(query_grad.astype(jnp.float32), axis=0).reshape(head_count, head_dim)
    key_b_grad = jnp.sum(key_grad.astype(jnp.float32), axis=0)[None, :]
    value_b_grad = jnp.sum(value_grad.astype(jnp.float32), axis=0)[None, :]
    query_w_grad = inner_prod(first_norm, query_grad)
    key_w_grad = inner_prod(first_norm, key_grad)
    value_w_grad = inner_prod(first_norm, value_grad)
    norm_one_grad = lax.psum(
        (
            times_trans(query_grad, w_query)
            + times_trans(key_grad, w_key)
            + times_trans(value_grad, value_weight_matrix)
        ).astype(jnp.bfloat16),
        "tp",
    ).astype(jnp.float32)
    input_part, gain_one_grad = norm_back(
        norm_one_grad, inputs, inv_one, gain_one.astype(jnp.float32)
    )
    input_grad = middle_grad + input_part
    full_grads = (
        gain_one_grad,
        query_w_grad,
        query_b_grad,
        key_w_grad,
        key_b_grad,
        value_w_grad,
        value_b_grad,
        out_w_grad,
        gain_two_grad,
        gate_w_grad,
        up_w_grad,
        down_grad,
    )
    shares = (
        lax.psum_scatter(
            full_grads[0].astype(jnp.bfloat16), "fsdp", scatter_dimension=0, tiled=True
        ).astype(jnp.float32),
        lax.psum_scatter(
            full_grads[1].astype(jnp.bfloat16), "fsdp", scatter_dimension=0, tiled=True
        ).astype(jnp.float32),
        lax.psum_scatter(
            full_grads[2].astype(jnp.bfloat16), "fsdp", scatter_dimension=1, tiled=True
        ).astype(jnp.float32),
        lax.psum_scatter(
            full_grads[3].astype(jnp.bfloat16), "fsdp", scatter_dimension=0, tiled=True
        ).astype(jnp.float32),
        lax.psum_scatter(
            full_grads[4].astype(jnp.bfloat16), "fsdp", scatter_dimension=1, tiled=True
        ).astype(jnp.float32),
        lax.psum_scatter(
            full_grads[5].astype(jnp.bfloat16), "fsdp", scatter_dimension=0, tiled=True
        ).astype(jnp.float32),
        lax.psum_scatter(
            full_grads[6].astype(jnp.bfloat16), "fsdp", scatter_dimension=1, tiled=True
        ).astype(jnp.float32),
        lax.psum_scatter(
            full_grads[7].astype(jnp.bfloat16), "fsdp", scatter_dimension=1, tiled=True
        ).astype(jnp.float32),
        lax.psum_scatter(
            full_grads[8].astype(jnp.bfloat16), "fsdp", scatter_dimension=0, tiled=True
        ).astype(jnp.float32),
        lax.psum_scatter(
            full_grads[9].astype(jnp.bfloat16), "fsdp", scatter_dimension=0, tiled=True
        ).astype(jnp.float32),
        lax.psum_scatter(
            full_grads[10].astype(jnp.bfloat16), "fsdp", scatter_dimension=0, tiled=True
        ).astype(jnp.float32),
        lax.psum_scatter(
            full_grads[11].astype(jnp.bfloat16), "fsdp", scatter_dimension=1, tiled=True
        ).astype(jnp.float32),
    )
    shares = (
        lax.psum(shares[0].astype(jnp.bfloat16), "ctx").astype(jnp.float32),
        lax.psum(shares[1].astype(jnp.bfloat16), "ctx").astype(jnp.float32),
        lax.psum(shares[2].astype(jnp.bfloat16), "ctx").astype(jnp.float32),
        lax.psum(shares[3].astype(jnp.bfloat16), "ctx").astype(jnp.float32),
        lax.psum(shares[4].astype(jnp.bfloat16), "ctx").astype(jnp.float32),
        lax.psum(shares[5].astype(jnp.bfloat16), "ctx").astype(jnp.float32),
        lax.psum(shares[6].astype(jnp.bfloat16), "ctx").astype(jnp.float32),
        lax.psum(shares[7].astype(jnp.bfloat16), "ctx").astype(jnp.float32),
        lax.psum(shares[8].astype(jnp.bfloat16), "ctx").astype(jnp.float32),
        lax.psum(shares[9].astype(jnp.bfloat16), "ctx").astype(jnp.float32),
        lax.psum(shares[10].astype(jnp.bfloat16), "ctx").astype(jnp.float32),
        lax.psum(shares[11].astype(jnp.bfloat16), "ctx").astype(jnp.float32),
    )
    return (
        layer_out[None],
        input_grad[None],
        shares[0],
        shares[1],
        shares[2],
        shares[3],
        shares[4],
        shares[5],
        shares[6],
        shares[7],
        shares[8],
        shares[9],
        shares[10],
        shares[11],
    )


def solution(mesh):
    placed = (
        P("fsdp", "ctx", None),
        P("fsdp", "ctx"),
        P("fsdp"),
        P("fsdp", "tp"),
        P("tp", "fsdp"),
        P("fsdp", "tp"),
        P("tp", "fsdp"),
        P("fsdp", "tp"),
        P("tp", "fsdp"),
        P("tp", "fsdp"),
        P("fsdp"),
        P("fsdp", "tp"),
        P("fsdp", "tp"),
        P("tp", "fsdp"),
        P("fsdp", "ctx", None),
    )
    return jax.shard_map(
        body,
        mesh=mesh,
        in_specs=placed,
        out_specs=(
            P("fsdp", "ctx", None),
            P("fsdp", "ctx", None),
            P("fsdp"),
            P("fsdp", "tp"),
            P("tp", "fsdp"),
            P("fsdp", "tp"),
            P("tp", "fsdp"),
            P("fsdp", "tp"),
            P("tp", "fsdp"),
            P("tp", "fsdp"),
            P("fsdp"),
            P("fsdp", "tp"),
            P("fsdp", "tp"),
            P("tp", "fsdp"),
        ),
        check_vma=False,
    )
```

profile of v0, /device:TPU:0, one launch (start us, length us, event | category | flops | bytes accessed | tf_op | source)
XLA Modules:
  0.0 1194.4 jit_solution(13074181225927293532)
XLA Ops:
  14.1 23.9 %all-reduce.10 = (bf16[64]{0:T(256)(128)(2,1)S(1)}, bf16[896]{0:T(1024)(128)(2,1)S(1)}, bf16[64]{0:T(256)(128)(2,1)S(1)}, bf16[896]{0:T(1024)(128)(2,1)}) all-reduce(bf16[64]{0:T(256)(128)(2,1)S(1)} %dynamic-update-slice.2, bf16[896]{0:T(1024)(128)(2,1)S(1)} %dynamic-update-slice, ...), channel_id=1, replica_groups=mesh['fsdp'=8,'ctx'=2,'tp'=2] {'fsdp'}, use_global_device_ids=true, to_apply=%add.2 | all-reduce | flops 1920 | bytes 7680
  40.0 30.8 %all-gather = bf16[8,112,64]{1,2,0:T(8,128)(2,1)S(1)} all-gather(bf16[1,112,64]{1,2,0:T(8,128)(2,1)} %bitcast.141), channel_id=1, replica_groups=mesh['fsdp'=8,'ctx'=2,'tp'=2] {'fsdp'}, dimensions={0}, use_global_device_ids=true | all-gather | bytes 129024 | tf_op jit(solution)/shard_map/all_gather | solution.py:74
  77.6 32.4 %all_gather.55 = bf16[896,448]{1,0:T(8,128)(2,1)S(1)} all-gather(bf16[112,448]{1,0:T(8,128)(2,1)S(1)} %copy-done.35), channel_id=1, replica_groups=mesh['fsdp'=8,'ctx'=2,'tp'=2] {'fsdp'}, dimensions={0}, use_global_device_ids=true | all-gather | bytes 903168 | tf_op jit(solution)/shard_map/all_gather | solution.py:72
  110.1 26.0 %all_gather.56 = bf16[7,64]{0,1:T(8,128)(2,1)S(1)} all-gather(bf16[7,8]{0,1:T(8,128)(2,1)S(1)} %copy.96), channel_id=1, replica_groups=mesh['fsdp'=8,'ctx'=2,'tp'=2] {'fsdp'}, dimensions={1}, use_global_device_ids=true | all-gather | bytes 1008 | tf_op jit(solution)/shard_map/all_gather | solution.py:73
  150.3 30.5 %all-gather.1 = bf16[8,112,64]{1,2,0:T(8,128)(2,1)S(1)} all-gather(bf16[1,112,64]{1,2,0:T(8,128)(2,1)S(1)} %bitcast.142), channel_id=1, replica_groups=mesh['fsdp'=8,'ctx'=2,'tp'=2] {'fsdp'}, dimensions={0}, use_global_device_ids=true | all-gather | bytes 129024 | tf_op jit(solution)/shard_map/all_gather | solution.py:76
  194.2 18.3 %conditional.2 = (f32[3584]{0:T(1024)S(1)}, f32[3584]{0:T(1024)S(1)}, f32[3584]{0:T(1024)S(1)}, f32[3584,64]{1,0:T(8,128)S(1)}) conditional(s32[]{:T(128)} %convert_element_type.267, (s32[512,7]{1,0:T(8,128)}, s32[512,7]{1,0:T(8,128)}, bf16[1024,128]{0,1:T(8,128)(2,1)S(1)}, bf16[3584,64]{1,0:T(8,128)(2,1)}) %tuple.35, () %tuple.36), branch_computations={%region_1.4_spmd, %region_4.5_spmd} | conditional | flops 1012920832 | bytes 46723104 | solution.py:145
  215.0 32.0 %all_gather.57 = bf16[448,896]{0,1:T(8,128)(2,1)S(1)} all-gather(bf16[448,112]{0,1:T(8,128)(2,1)S(1)} %copy.105), channel_id=1, replica_groups=mesh['fsdp'=8,'ctx'=2,'tp'=2] {'fsdp'}, dimensions={1}, use_global_device_ids=true | all-gather | bytes 903168 | tf_op jit(solution)/shard_map/all_gather | solution.py:78
  250.6 15.1 %all-reduce.19.cloned.1.call-done = bf16[512,896]{1,0:T(8,128)(2,1)} async-done(((bf16[512,896]{1,0:T(8,128)(2,1)}), bf16[512,896]{1,0:T(8,128)(2,1)}) %all-reduce.19.cloned.1.call-update) | async-done | bytes 917520 | tf_op jit(solution)/shard_map/psum | solution.py:151
  268.7 55.2 %all-gather.6.cloned.1.call-done = bf16[896,2432]{1,0:T(8,128)(2,1)} async-done(((bf16[112,2432]{1,0:T(8,128)(2,1)}), bf16[896,2432]{1,0:T(8,128)(2,1)}) %all-gather.6.cloned.1.call-update) | async-done | bytes 4358160 | tf_op jit(solution)/shard_map/all_gather | solution.py:82
  323.9 6.8 fusion.82
  330.7 68.9 %all-gather.8.cloned.1.call-done = bf16[896,2432]{1,0:T(8,128)(2,1)} async-done(((bf16[112,2432]{1,0:T(8,128)(2,1)}), bf16[896,2432]{1,0:T(8,128)(2,1)}) %all-gather.8.cloned.1.call-update) | async-done | bytes 4358160 | tf_op jit(solution)/shard_map/all_gather | solution.py:83
  399.5 7.6 fusion.83
  407.2 68.0 %all-gather.10.cloned.1.call-done = bf16[2432,896]{0,1:T(8,128)(2,1)} async-done(((bf16[2432,112]{0,1:T(8,128)(2,1)}), bf16[2432,896]{0,1:T(8,128)(2,1)}) %all-gather.10.cloned.1.call-update) | async-done | bytes 4358160 | tf_op jit(solution)/shard_map/all_gather | solution.py:84
  475.2 8.3 multiply_convert_fusion.1
  483.5 6.9 fusion.84
  494.4 17.9 %all-reduce.21.cloned.1.call-done = bf16[512,896]{1,0:T(8,128)(2,1)} async-done(((bf16[512,896]{1,0:T(8,128)(2,1)}), bf16[512,896]{1,0:T(8,128)(2,1)}) %all-reduce.21.cloned.1.call-update) | async-done | bytes 917520 | tf_op jit(solution)/shard_map/psum | solution.py:186
  517.9 36.6 %conditional.3 = (bf16[1024,128]{0,1:T(8,128)(2,1)S(1)}, f32[512,448]{0,1:T(8,128)S(1)}, f32[512,7,64]{0,2,1:T(8,128)}) conditional(s32[]{:T(128)} %convert_element_type.267, (s32[512,7]{1,0:T(8,128)}, s32[512,7]{1,0:T(8,128)}, bf16[1024,128]{0,1:T(8,128)(2,1)S(1)}, bf16[3584,64]{1,0:T(8,128)(2,1)S(1)}, f32[3584]{0:T(1024)S(1)}, ...), branch_computations={%region_10.0_spmd, %region_12.13_spmd} | conditional | flops 2390392832 | bytes 129343664 | solution.py:220
  520.6 9.4 exponential_select_fusion.1
  532.9 7.5 multiply_convert_fusion
  576.8 6.4 convolution_convert_fusion
  583.3 6.9 convolution_convert_fusion.3
  600.8 34.3 %reduce-scatter.32.cloned.1.call-done = bf16[112,448]{1,0:T(8,128)(2,1)} async-done(((bf16[896,448]{1,0:T(8,128)(2,1)}), bf16[112,448]{1,0:T(8,128)(2,1)}) %reduce-scatter.32.cloned.1.call-update) | async-done | bytes 100368
  636.8 64.0 %reduce-scatter.20.cloned.1.call-done = bf16[112,448]{1,0:T(8,128)(2,1)} async-done(((bf16[896,448]{1,0:T(8,128)(2,1)}), bf16[112,448]{1,0:T(8,128)(2,1)}) %reduce-scatter.20.cloned.1.call-update) | async-done | bytes 100368 | tf_op jit(solution)/shard_map/reduce_scatter | solution.py:273
  700.8 92.5 %reduce-scatter.24.cloned.1.call-done = bf16[112,2432]{1,0:T(8,128)(2,1)} async-done(((bf16[896,2432]{1,0:T(8,128)(2,1)}), bf16[112,2432]{1,0:T(8,128)(2,1)}) %reduce-scatter.24.cloned.1.call-update) | async-done | bytes 544784 | tf_op jit(solution)/shard_map/reduce_scatter | solution.py:300
  793.3 92.2 %reduce-scatter.22.cloned.1.call-done = bf16[112,2432]{1,0:T(8,128)(2,1)} async-done(((bf16[896,2432]{1,0:T(8,128)(2,1)}), bf16[112,2432]{1,0:T(8,128)(2,1)}) %reduce-scatter.22.cloned.1.call-update) | async-done | bytes 544784 | tf_op jit(solution)/shard_map/reduce_scatter | solution.py:297
  885.5 92.3 %reduce-scatter.26.cloned.1.call-done = bf16[2432,112]{0,1:T(8,128)(2,1)} async-done(((bf16[2432,896]{0,1:T(8,128)(2,1)}), bf16[2432,112]{0,1:T(8,128)(2,1)}) %reduce-scatter.26.cloned.1.call-update) | async-done | bytes 544784 | tf_op jit(solution)/shard_map/reduce_scatter | solution.py:303
  979.1 56.4 %reduce-scatter.28.cloned.1.call-done = bf16[112,64]{1,0:T(8,128)(2,1)} async-done(((bf16[896,64]{1,0:T(8,128)(2,1)}), bf16[112,64]{1,0:T(8,128)(2,1)}) %reduce-scatter.28.cloned.1.call-update) | async-done | bytes 14352
  1036.3 56.2 %reduce-scatter.30.cloned.1.call-done = bf16[112,64]{1,0:T(8,128)(2,1)} async-done(((bf16[896,64]{1,0:T(8,128)(2,1)}), bf16[112,64]{1,0:T(8,128)(2,1)}) %reduce-scatter.30.cloned.1.call-update) | async-done | bytes 14352
  1093.4 22.8 %all-reduce.23.cloned.1.call-done = (bf16[512,896]{1,0:T(8,128)(2,1)}, bf16[512,896]{1,0:T(8,128)(2,1)}) async-done(((bf16[512,896]{1,0:T(8,128)(2,1)}, bf16[512,896]{1,0:T(8,128)(2,1)}), (bf16[512,896]{1,0:T(8,128)(2,1)}, bf16[512,896]{1,0:T(8,128)(2,1)})) %all-reduce.23.cloned.1.call-update) | async-done | bytes 1835024 | tf_op jit(solution)/shard_map/psum | solution.py:162
  1118.2 21.9 %all-reduce.9 = (bf16[896]{0:T(1024)(128)(2,1)S(1)}, bf16[7,64]{1,0:T(8,128)(2,1)S(1)}, bf16[1,64]{1,0:T(2,128)(2,1)S(1)}, bf16[1,64]{1,0:T(2,128)(2,1)S(1)}, bf16[896]{0:T(1024)(128)(2,1)S(1)}) all-reduce(bf16[896]{0:T(1024)(128)(2,1)S(1)} %get-tuple-element.173, ...), channel_id=3, replica_groups=mesh['fsdp'=8,'ctx'=2,'tp'=2] {'fsdp'}, use_global_device_ids=true, to_apply=%region_17.18.clone | all-reduce | flops 2368 | bytes 9472
  1140.4 8.9 all-reduce.12
  1157.2 22.6 %all-reduce.25.cloned.1.call-done = (bf16[112,448]{1,0:T(8,128)(2,1)}, bf16[448,112]{1,0:T(8,128)(2,1)}, bf16[112,2432]{1,0:T(8,128)(2,1)}, bf16[112,2432]{1,0:T(8,128)(2,1)}, bf16[2432,112]{0,1:T(8,128)(2,1)}) async-done(((bf16[112,448]{1,0:T(8,128)(2,1)}, bf16[448,112]{1,0:T(8,128)(2,1)}, bf16[112,2432]{1,0:T(8,128)(2,1)}, bf16[112,2432]{1,0:T(8,128)(2,1)}, bf16[2432,112]{0,1:T(8,128)(2,1)}), ...) | async-done | bytes 1835024 | tf_op jit(solution)/shard_map/psum | solution.py:309
  (271 shorter events, 150.3 us)
Async XLA Ops:
  8.0 257.6 %all-reduce.19.cloned.1.call-start = ((), (), s32[]{:S(2)}) async-start(), calls=%async_computation.8 | async-start | bytes 1835008 | tf_op jit(solution)/shard_map/psum | solution.py:151
  38.0 143.1 %copy-start.40 = (f32[896]{0:T(1024)}, f32[896]{0:T(1024)S(1)}, u32[]{:S(2)}) copy-start(f32[896]{0:T(1024)S(1)} %convert_element_type.268) | copy-start | bytes 10756
  40.0 141.1 %copy-start.42 = (f32[512]{0:T(512)}, f32[512]{0:T(512)S(1)}, u32[]{:S(2)}) copy-start(f32[512]{0:T(512)S(1)} %get-tuple-element.224) | copy-start | bytes 6148
  76.2 33.9 %copy-start.48 = (bf16[7,8]{1,0:T(8,128)(2,1)S(1)}, bf16[7,8]{1,0:T(8,128)(2,1)}, u32[]{:S(2)}) copy-start(bf16[7,8]{1,0:T(8,128)(2,1)} %param.23) | copy-start | bytes 340
  76.2 60.1 %copy-start = (bf16[1,512,896]{2,1,0:T(8,128)(2,1)S(1)}, bf16[1,512,896]{2,1,0:T(8,128)(2,1)}, u32[]{:S(2)}) copy-start(bf16[1,512,896]{2,1,0:T(8,128)(2,1)} %param.19) | copy-start | bytes 2752516
  110.0 28.4 %copy-start.11 = (bf16[896,448]{1,0:T(8,128)(2,1)}, bf16[896,448]{1,0:T(8,128)(2,1)S(1)}, u32[]{:S(2)}) copy-start(bf16[896,448]{1,0:T(8,128)(2,1)S(1)} %all_gather.55) | copy-start | bytes 2408452
  147.5 40.5 %copy-start.45 = (s32[1,512]{1,0:T(1,128)S(1)}, s32[1,512]{1,0:T(1,128)}, u32[]{:S(2)}) copy-start(s32[1,512]{1,0:T(1,128)} %param.20) | copy-start | bytes 6148
  147.5 40.5 %copy-start.5 = (f32[3584,64]{1,0:T(8,128)S(1)}, f32[3584,64]{1,0:T(8,128)}, u32[]{:S(2)}) copy-start(f32[3584,64]{1,0:T(8,128)} %mul.271) | copy-start | bytes 2752516
  214.9 34.4 %copy-start.15 = (bf16[512,448]{1,0:T(8,128)(2,1)}, bf16[512,448]{1,0:T(8,128)(2,1)S(1)}, u32[]{:S(2)}) copy-start(bf16[512,448]{1,0:T(8,128)(2,1)S(1)} %reshape.231) | copy-start | bytes 1376260
  248.7 75.2 %all-gather.6.cloned.1.call-start = ((), (), s32[]{:S(2)}) async-start(), calls=%async_computation.9 | async-start | bytes 4902912 | tf_op jit(solution)/shard_map/all_gather | solution.py:82
  249.3 150.2 %all-gather.8.cloned.1.call-start = ((), (), s32[]{:S(2)}) async-start(), calls=%async_computation.10 | async-start | bytes 4902912 | tf_op jit(solution)/shard_map/all_gather | solution.py:83
  249.9 225.3 %all-gather.10.cloned.1.call-start = ((), (), s32[]{:S(2)}) async-start(), calls=%async_computation.11 | async-start | bytes 4902912 | tf_op jit(solution)/shard_map/all_gather | solution.py:84
  250.5 261.8 %all-reduce.21.cloned.1.call-start = ((), (), s32[]{:S(2)}) async-start(), calls=%async_computation.12 | async-start | bytes 1835008 | tf_op jit(solution)/shard_map/psum | solution.py:186
  268.7 55.2 %copy-start.25 = (bf16[512,896]{1,0:T(8,128)(2,1)}, bf16[512,896]{1,0:T(8,128)(2,1)S(1)}, u32[]{:S(2)}) copy-start(bf16[512,896]{1,0:T(8,128)(2,1)S(1)} %multiply_convert_fusion.4) | copy-start | bytes 2752516
  330.7 144.5 %copy-start.22 = (bf16[1,512,896]{2,1,0:T(8,128)(2,1)S(1)}, bf16[1,512,896]{2,1,0:T(8,128)(2,1)}, u32[]{:S(2)}) copy-start(bf16[1,512,896]{2,1,0:T(8,128)(2,1)} %param.33) | copy-start | bytes 2752516
  490.5 21.8 %copy-start.3 = (bf16[512,896]{1,0:T(8,128)(2,1)S(1)}, bf16[512,896]{1,0:T(8,128)(2,1)}, u32[]{:S(2)}) copy-start(bf16[512,896]{1,0:T(8,128)(2,1)} %all-reduce.19.cloned.1.call-done) | copy-start | bytes 2752516
  494.3 96.2 %reduce-scatter.18.cloned.1.call-start = ((), (), s32[]{:S(2)}) async-start(), calls=%async_computation.13 | async-start | bytes 393216 | tf_op jit(solution)/shard_map/reduce_scatter | solution.py:223
  517.9 12.1 %copy-start.7 = (bf16[3584,64]{1,0:T(8,128)(2,1)}, bf16[3584,64]{1,0:T(8,128)(2,1)S(1)}, u32[]{:S(2)}) copy-start(bf16[3584,64]{1,0:T(8,128)(2,1)S(1)} %get-tuple-element.74) | copy-start | bytes 1376260 | tf_op jit(solution)/shard_map/cond
  532.9 10.5 slice-start
  532.9 10.5 slice-start.1
  532.9 10.5 slice-start.2
  555.7 79.4 %reduce-scatter.32.cloned.1.call-start = ((), (), s32[]{:S(2)}) async-start(), calls=%async_computation.20 | async-start | bytes 1032192
  559.7 141.1 %reduce-scatter.20.cloned.1.call-start = ((), (), s32[]{:S(2)}) async-start(), calls=%async_computation.14 | async-start | bytes 1032192 | tf_op jit(solution)/shard_map/reduce_scatter | solution.py:273
  562.6 230.7 %reduce-scatter.24.cloned.1.call-start = ((), (), s32[]{:S(2)}) async-start(), calls=%async_computation.16 | async-start | bytes 4902912 | tf_op jit(solution)/shard_map/reduce_scatter | solution.py:300
  569.2 316.3 %reduce-scatter.22.cloned.1.call-start = ((), (), s32[]{:S(2)}) async-start(), calls=%async_computation.15 | async-start | bytes 4902912 | tf_op jit(solution)/shard_map/reduce_scatter | solution.py:297
  575.6 402.2 %reduce-scatter.26.cloned.1.call-start = ((), (), s32[]{:S(2)}) async-start(), calls=%async_computation.17 | async-start | bytes 4902912 | tf_op jit(solution)/shard_map/reduce_scatter | solution.py:303
  583.2 452.2 %reduce-scatter.28.cloned.1.call-start = ((), (), s32[]{:S(2)}) async-start(), calls=%async_computation.18 | async-start | bytes 258048
  596.7 495.8 %reduce-scatter.30.cloned.1.call-start = ((), (), s32[]{:S(2)}) async-start(), calls=%async_computation.19 | async-start | bytes 258048
  597.3 518.9 %all-reduce.23.cloned.1.call-start = ((), (), s32[]{:S(2)}) async-start(), calls=%async_computation.21 | async-start | bytes 3670016 | tf_op jit(solution)/shard_map/psum | solution.py:162
  600.5 552.6 %copy-start.2 = (f32[512,896]{1,0:T(8,128)S(1)}, f32[512,896]{1,0:T(8,128)}, u32[]{:S(2)}) copy-start(f32[512,896]{1,0:T(8,128)} %copy-done.1) | copy-start | bytes 5505028
  600.5 552.6 %copy-start.46 = (f32[512]{0:T(512)S(1)}, f32[512]{0:T(512)}, u32[]{:S(2)}) copy-start(f32[512]{0:T(512)} %get-tuple-element.223) | copy-start | bytes 6148
  600.5 579.3 %all-reduce.25.cloned.1.call-start = ((), (), s32[]{:S(2)}) async-start(), calls=%async_computation.22 | async-start | bytes 3727360 | tf_op jit(solution)/shard_map/psum | solution.py:309
  (39 other events, 115.3 us)
Sparse Core Ops, SparseCore 0:
  248.9 16.7 all-reduce.18
  494.4 17.8 all-reduce.20
  555.8 12.8 reduce-scatter.17
  572.2 62.8 reduce-scatter.31
  638.9 61.9 reduce-scatter.19
  704.6 88.6 reduce-scatter.23
  797.2 88.2 reduce-scatter.21
  889.4 88.3 reduce-scatter.25
  981.8 53.5 reduce-scatter.27
  1039.1 53.4 reduce-scatter.29
  1096.2 19.9 all-reduce.22
  1119.2 60.5 all-reduce.24
Sparse Core Ops, SparseCore 1:
  251.6 72.2 all-gather.5
  326.2 73.3 all-gather.7
  401.8 73.3 all-gather.9
where the time goes:
time: 1200 us; the launch traced here: 1190 us
  waiting for transfers between devices  760 us (63%)
  blocking collectives  213 us (18%)
  matrix products  108 us (9%)
  local copies, waits for them, and re-layouts  49 us (4%)
  other arithmetic  43.8 us (4%)
  between operations  19.4 us (2%)
    unnamed x18, waiting for transfers between devices  149 us
    reduce_scatter x1, waiting for transfers between devices, body(): lax.psum_scatter(full_grads[10].astype(jnp.bfloat16), 'fsdp', scatter_dim...  92.5 us
    reduce_scatter x1, waiting for transfers between devices, body(): lax.psum_scatter(full_grads[11].astype(jnp.bfloat16), 'fsdp', scatter_dim...  92.3 us
    reduce_scatter x1, waiting for transfers between devices, body(): lax.psum_scatter(full_grads[9].astype(jnp.bfloat16), 'fsdp', scatter_dime...  92.2 us
    all_gather x1, waiting for transfers between devices, body(): lax.all_gather(up_weight, 'fsdp', axis=0, tiled=True)  68.9 us
    all_gather x1, waiting for transfers between devices, body(): lax.all_gather(down_weight, 'fsdp', axis=1, tiled=True)  68 us
    reduce_scatter x1, waiting for transfers between devices, body(): lax.psum_scatter(full_grads[1].astype(jnp.bfloat16), 'fsdp', scatter_dime...  64 us
    all_gather x1, waiting for transfers between devices, body(): lax.all_gather(gate_weight, 'fsdp', axis=0, tiled=True)  55.2 us
  transfers between devices with their start and end apart: 15, of which 14 were waited for; matrix products, arithmetic and copies ran while one was open for 6% of the time, Pallas kernels for 0%

commit v1 on v0

v1 whole, which is shorter than its diff:
```python
import jax
import jax.numpy as jnp
from jax import lax
from jax.sharding import PartitionSpec as P

NORM_EPS = 1e-06
MASK_FILL = -1e30
SMALL_ROWS = 16


def product(left, right):
    return jnp.dot(left, right, preferred_element_type=jnp.float32)


def inner_prod(left, right):
    return lax.dot_general(
        left, right, (((0,), (0,)), ((), ())), preferred_element_type=jnp.float32
    )


def times_trans(left, right):
    return lax.dot_general(
        left, right, (((1,), (1,)), ((), ())), preferred_element_type=jnp.float32
    )


def low(value):
    return value.astype(jnp.bfloat16)


def wide(value):
    return value.astype(jnp.float32)


def rotary_apply(tensor, cosine_table, sine_table):
    half_dim = tensor.shape[-1] // 2
    turned = jnp.concatenate([-tensor[..., half_dim:], tensor[..., :half_dim]], axis=-1)
    return tensor * cosine_table + turned * sine_table


def unrotate(upstream, cosine_table, sine_table):
    half_dim = upstream.shape[-1] // 2
    shifted = upstream * sine_table
    turned_back = jnp.concatenate([shifted[..., half_dim:], -shifted[..., :half_dim]], axis=-1)
    return upstream * cosine_table + turned_back


def norm_back(upstream, source, inverse, gain_vec):
    scaled = upstream * gain_vec
    gain_grad = jnp.sum(upstream * source * inverse, axis=0)
    input_part = inverse * scaled - source * inverse**3 * jnp.mean(
        scaled * source, axis=-1, keepdims=True
    )
    return (input_part, gain_grad)


def fsdp_place():
    index = lax.axis_index("fsdp")
    return index // 2, index % 2


def gather_pieces(shard):
    count = lax.axis_size("fsdp")
    depth = count // 2
    below, above = [shard], [shard]
    below_x = [lax.ppermute(shard, "fsdp", [(i, i ^ 1) for i in range(count)])]
    above_x = [below_x[0]]
    for step in range(1, depth):
        below.append(
            lax.ppermute(
                below[-1], "fsdp", [(i, i + 2) for i in range(count - 2) if i // 2 >= step - 1]
            )
        )
        above.append(
            lax.ppermute(
                above[-1],
                "fsdp",
                [(i, i - 2) for i in range(2, count) if i // 2 + step - 1 < depth],
            )
        )
        below_x.append(
            lax.ppermute(
                below[-1], "fsdp", [(i, i ^ 1) for i in range(count) if i // 2 >= step]
            )
        )
        above_x.append(
            lax.ppermute(
                above[-1], "fsdp", [(i, i ^ 1) for i in range(count) if i // 2 + step < depth]
            )
        )
    return below, above, below_x, above_x


def assemble(pieces, first, rows):
    count = lax.axis_size("fsdp")
    depth = count // 2
    z, x = fsdp_place()
    below, above, below_x, above_x = pieces
    cols = below[0].shape[1]
    full = jnp.zeros((count * rows, cols), below[0].dtype)

    def cut(value):
        return value[first : first + rows]

    for distance in range(depth):
        at = lax.rem(z + distance, depth)
        for up_list, down_list, side in ((above, below, x), (above_x, below_x, 1 - x)):
            if distance == 0:
                piece = cut(up_list[0])
            else:
                piece = jnp.where(
                    z + distance < depth, cut(up_list[distance]), cut(down_list[depth - distance])
                )
            full = lax.dynamic_update_slice(full, piece, ((2 * at + side) * rows, 0))
    return full


def scatter_sum(full):
    count = lax.axis_size("fsdp")
    depth = count // 2
    z, x = fsdp_place()

    def block(target, side):
        return lax.dynamic_index_in_dim(full, 2 * target + side, 0, keepdims=False)

    def pair_sum(target, pairs):
        return wide(block(target, x)) + wide(lax.ppermute(block(target, 1 - x), "fsdp", pairs))

    up = down = None
    for distance in range(depth - 1, 0, -1):
        valid_up = [i for i in range(count) if i // 2 + distance < depth]
        valid_down = [i for i in range(count) if i // 2 >= distance]
        sum_up = pair_sum(jnp.minimum(z + distance, depth - 1), [(i, i ^ 1) for i in valid_up])
        sum_down = pair_sum(jnp.maximum(z - distance, 0), [(i, i ^ 1) for i in valid_down])
        if up is not None:
            sum_up = sum_up + wide(up)
            sum_down = sum_down + wide(down)
        up = lax.ppermute(low(sum_up), "fsdp", [(i, i + 2) for i in valid_up])
        down = lax.ppermute(low(sum_down), "fsdp", [(i, i - 2) for i in valid_down])
    total = pair_sum(z, [(i, i ^ 1) for i in range(count)])
    if up is not None:
        total = total + wide(up) + wide(down)
    return total


def swap_cores(value):
    count = lax.axis_size("tp")
    return lax.ppermute(value, "tp", [(i, (i + 1) % count) for i in range(count)])


def from_ctx(value, ahead):
    count = lax.axis_size("ctx")
    return lax.ppermute(value, "ctx", [((i + ahead) % count, i) for i in range(count)])


def to_ctx(value, ahead):
    count = lax.axis_size("ctx")
    return lax.ppermute(value, "ctx", [(i, (i + ahead) % count) for i in range(count)])


def half_rows(value, which):
    rows = value.shape[0] // 2
    return lax.dynamic_slice_in_dim(value, which * rows, rows, 0)


def join_halves(mine, others, core):
    return jnp.concatenate(
        [jnp.where(core == 0, mine, others), jnp.where(core == 0, others, mine)], axis=0
    )


def ctx_blocks(value, core):
    blocks = []
    mine = half_rows(value, core)
    for ahead in range(1, lax.axis_size("ctx")):
        got = from_ctx(mine, ahead)
        blocks.append(join_halves(got, swap_cores(got), core))
    return blocks


def core_sum(value, core):
    return low(wide(half_rows(value, core)) + wide(swap_cores(half_rows(value, 1 - core))))


def block_sums(own, others, core):
    sent = [to_ctx(core_sum(other, core), ahead + 1) for ahead, other in enumerate(others)]
    total = wide(core_sum(own, core))
    for part in sent:
        total = total + wide(part)
    total = low(total)
    return join_halves(total, swap_cores(total), core)


def pick(choices, index):
    out = choices[0]
    for number, choice in enumerate(choices[1:], 1):
        out = jnp.where(index == number, choice, out)
    return out


def body(
    tokens,
    positions,
    norm1_gain,
    q_weight,
    q_bias,
    key_projection,
    key_bias,
    value_projection,
    value_bias,
    o_weight,
    norm2_gain,
    gate_weight,
    up_weight,
    down_weight,
    out_grad,
):
    row_count, width = tokens.shape[1:]
    shards = lax.axis_size("fsdp")
    ctx_count = lax.axis_size("ctx")
    ctx = lax.axis_index("ctx")
    core = lax.axis_index("tp")
    head_dim = key_projection.shape[1]
    head_count = q_weight.shape[1] // head_dim
    q_cols = head_count * head_dim
    query_rows = row_count * head_count
    score_scale = head_dim ** (-0.5)
    shard_rows = q_weight.shape[0]
    hidden_cols = gate_weight.shape[1] // ctx_count
    bias_cols = q_bias.shape[1]

    small = jnp.concatenate(
        [norm1_gain, norm2_gain, q_bias.reshape(-1), key_bias.reshape(-1), value_bias.reshape(-1)]
    )
    qkv_shard = jnp.concatenate([q_weight, key_projection, value_projection], axis=1)
    qkv_cols = qkv_shard.shape[1]
    small_row = jnp.pad(small[None, :], ((0, SMALL_ROWS - 1), (0, qkv_cols - small.shape[0])))
    attn_shard = jnp.concatenate([qkv_shard, small_row], axis=0)
    attn_pieces = gather_pieces(attn_shard)
    w_qkv = assemble(attn_pieces, 0, shard_rows)
    small_full = assemble(attn_pieces, shard_rows, SMALL_ROWS).reshape(
        shards, SMALL_ROWS, qkv_cols
    )[:, 0]
    gain_one = small_full[:, :shard_rows].reshape(-1)
    gain_two = small_full[:, shard_rows : 2 * shard_rows].reshape(-1)
    at = 2 * shard_rows
    b_query = (
        small_full[:, at : at + head_count * bias_cols]
        .reshape(shards, head_count, bias_cols)
        .transpose(1, 0, 2)
        .reshape(-1)
    )
    at += head_count * bias_cols
    b_key = small_full[:, at : at + bias_cols].reshape(-1)
    b_value = small_full[:, at + bias_cols : at + 2 * bias_cols].reshape(-1)
    b_qkv = jnp.concatenate([b_query, b_key, b_value])

    o_trans = assemble(gather_pieces(o_weight.T), 0, shard_rows)

    def my_columns(weight):
        return pick(
            [weight[:, i * hidden_cols : (i + 1) * hidden_cols] for i in range(ctx_count)], ctx
        )

    w_gate = assemble(gather_pieces(my_columns(gate_weight)), 0, shard_rows)
    w_up = assemble(gather_pieces(my_columns(up_weight)), 0, shard_rows)
    down_trans = assemble(gather_pieces(my_columns(down_weight.T)), 0, shard_rows)

    grad_low = out_grad[0]
    grad_others = ctx_blocks(grad_low, core)

    first_row = ctx * row_count
    inputs = wide(tokens[0])
    seq_positions = positions[0]
    token_index = first_row + jnp.arange(row_count, dtype=jnp.int32)
    doc_start = token_index - seq_positions
    query_index = jnp.repeat(token_index, head_count)
    query_begin = jnp.repeat(doc_start, head_count)
    key_index = jnp.concatenate(
        [
            lax.rem(ctx + ahead, ctx_count) * row_count + jnp.arange(row_count, dtype=jnp.int32)
            for ahead in range(ctx_count)
        ]
    )
    inv_freq = 1000000.0 ** (-jnp.arange(0, head_dim, 2, dtype=jnp.float32) / head_dim)
    angles = wide(seq_positions)[:, None] * inv_freq[None, :]
    angles = jnp.concatenate([angles, angles], axis=-1)
    cosine_table = jnp.cos(angles)
    sine_table = jnp.sin(angles)
    inv_one = lax.rsqrt(jnp.mean(inputs * inputs, axis=-1, keepdims=True) + NORM_EPS)
    first_norm = low(inputs * inv_one * wide(gain_one))
    qkv_lin = product(first_norm, w_qkv) + wide(b_qkv)
    value_matrix = low(qkv_lin[:, q_cols + head_dim :])
    key_rows = low(rotary_apply(qkv_lin[:, q_cols : q_cols + head_dim], cosine_table, sine_table))
    key_value = jnp.concatenate([key_rows, value_matrix], axis=1)
    kv_all = jnp.concatenate(
        [key_value] + [from_ctx(key_value, ahead) for ahead in range(1, ctx_count)], axis=0
    )
    query_matrix = low(
        rotary_apply(
            qkv_lin[:, :q_cols].reshape(row_count, head_count, head_dim),
            cosine_table[:, None, :],
            sine_table[:, None, :],
        )
    ).reshape(query_rows, head_dim)
    key_part = kv_all[:, :head_dim]
    value_part = kv_all[:, head_dim:]
    visible = (key_index[None, :] <= query_index[:, None]) & (
        key_index[None, :] >= query_begin[:, None]
    )
    scores = times_trans(query_matrix, key_part) * score_scale
    top_score = jnp.max(jnp.where(visible, scores, MASK_FILL), axis=1)
    weights = jnp.where(visible, jnp.exp(scores - top_score[:, None]), 0.0)
    weight_sum = jnp.sum(weights, axis=1)
    partial_value = product(low(weights), value_part)
    log_total = top_score + jnp.log(weight_sum)
    attn_full = partial_value / weight_sum[:, None]
    attn_low = low(attn_full).reshape(row_count, q_cols)
    out_part = low(times_trans(attn_low, o_trans))
    middle = inputs + (wide(out_part) + wide(swap_cores(out_part)))
    inv_two = lax.rsqrt(jnp.mean(middle * middle, axis=-1, keepdims=True) + NORM_EPS)
    norm_two = low(middle * inv_two * wide(gain_two))
    norm_blocks = [norm_two] + ctx_blocks(norm_two, core)
    grad_blocks = [grad_low] + grad_others

    hidden_blocks, gate_grads, up_grads, norm_parts, down_parts = [], [], [], [], []
    for norm_block, grad_block in zip(norm_blocks, grad_blocks):
        hidden_grad = product(grad_block, down_trans)
        gate_proj = product(norm_block, w_gate)
        up_proj = product(norm_block, w_up)
        sigmoid_gate = jax.nn.sigmoid(gate_proj)
        silu_gate = gate_proj * sigmoid_gate
        hidden_blocks.append(low(silu_gate * up_proj))
        gate_grads.append(
            low(hidden_grad * up_proj * sigmoid_gate * (1.0 + gate_proj * (1.0 - sigmoid_gate)))
        )
        up_grads.append(low(hidden_grad * silu_gate))
        norm_parts.append(
            low(times_trans(gate_grads[-1], w_gate) + times_trans(up_grads[-1], w_up))
        )
        down_parts.append(low(times_trans(hidden_blocks[-1], down_trans)))
    norm_two_grad = wide(block_sums(norm_parts[0], norm_parts[1:], core))
    layer_out = low(middle + wide(block_sums(down_parts[0], down_parts[1:], core)))
    norm_all = jnp.concatenate(norm_blocks, axis=0)
    grad_all = jnp.concatenate(grad_blocks, axis=0)

    def ff_share(weight_grad):
        share = scatter_sum(low(weight_grad).reshape(shards, shard_rows, hidden_cols))
        low_share = low(share)
        parts = [low_share] + [from_ctx(low_share, ahead) for ahead in range(1, ctx_count)]
        return jnp.concatenate(
            [wide(pick(parts, lax.rem(i - ctx + ctx_count, ctx_count))) for i in range(ctx_count)],
            axis=1,
        )

    gate_share = ff_share(inner_prod(norm_all, jnp.concatenate(gate_grads, axis=0)))
    up_share = ff_share(inner_prod(norm_all, jnp.concatenate(up_grads, axis=0)))
    down_share = ff_share(inner_prod(grad_all, jnp.concatenate(hidden_blocks, axis=0))).T

    grad_top = wide(grad_low)
    middle_part, gain_two_grad = norm_back(norm_two_grad, middle, inv_two, wide(gain_two))
    middle_grad = grad_top + middle_part
    middle_low = low(middle_grad)
    attn_grad = low(product(middle_low, o_trans)).reshape(query_rows, head_dim)
    row_delta = jnp.sum(wide(attn_grad) * attn_full, axis=1)
    probabilities = jnp.where(visible, jnp.exp(scores - log_total[:, None]), 0.0)
    prob_grad = times_trans(attn_grad, value_part)
    score_grad = low(probabilities * (prob_grad - row_delta[:, None]) * score_scale)
    key_part_grad = inner_prod(score_grad, query_matrix)
    value_part_grad = inner_prod(low(probabilities), attn_grad)
    pair_grad = low(jnp.concatenate([key_part_grad, value_part_grad], axis=1))
    pair_mine = wide(pair_grad[:row_count])
    for ahead in range(1, ctx_count):
        pair_mine = pair_mine + wide(
            to_ctx(pair_grad[ahead * row_count : (ahead + 1) * row_count], ahead)
        )
    query_acc = product(score_grad, key_part)
    key_grad = low(unrotate(pair_mine[:, :head_dim], cosine_table, sine_table))
    value_grad = low(pair_mine[:, head_dim:])
    query_grad = low(
        unrotate(
            query_acc.reshape(row_count, head_count, head_dim),
            cosine_table[:, None, :],
            sine_table[:, None, :],
        )
    ).reshape(row_count, q_cols)
    qkv_grad = jnp.concatenate([query_grad, key_grad, value_grad], axis=1)
    bias_grad = low(jnp.sum(wide(qkv_grad), axis=0))
    qkv_w_grad = inner_prod(first_norm, qkv_grad)
    norm_one_part = low(times_trans(qkv_grad, w_qkv))
    norm_one_grad = wide(norm_one_part) + wide(swap_cores(norm_one_part))
    input_part, gain_one_grad = norm_back(norm_one_grad, inputs, inv_one, wide(gain_one))
    input_grad = middle_grad + input_part

    small_grad = jnp.concatenate(
        [
            low(gain_one_grad).reshape(shards, shard_rows),
            low(gain_two_grad).reshape(shards, shard_rows),
            bias_grad[:q_cols]
            .reshape(head_count, shards, bias_cols)
            .transpose(1, 0, 2)
            .reshape(shards, head_count * bias_cols),
            bias_grad[q_cols : q_cols + head_dim].reshape(shards, bias_cols),
            bias_grad[q_cols + head_dim :].reshape(shards, bias_cols),
        ],
        axis=1,
    )
    small_grad = jnp.pad(
        small_grad[:, None, :],
        ((0, 0), (0, SMALL_ROWS - 1), (0, qkv_cols - small_grad.shape[1])),
    )

    def ctx_sum(value):
        value = low(value)
        total = wide(value)
        for ahead in range(1, ctx_count):
            total = total + wide(from_ctx(value, ahead))
        return total

    o_share = ctx_sum(
        scatter_sum(low(inner_prod(middle_low, attn_low)).reshape(shards, shard_rows, q_cols))
    ).T
    attn_share = ctx_sum(
        scatter_sum(
            jnp.concatenate(
                [low(qkv_w_grad).reshape(shards, shard_rows, qkv_cols), small_grad], axis=1
            )
        )
    )
    small_share = attn_share[shard_rows]
    at = 2 * shard_rows
    q_bias_end = at + head_count * bias_cols
    return (
        layer_out[None],
        input_grad[None],
        small_share[:shard_rows],
        attn_share[:shard_rows, :q_cols],
        small_share[at:q_bias_end].reshape(head_count, bias_cols),
        attn_share[:shard_rows, q_cols : q_cols + head_dim],
        small_share[q_bias_end : q_bias_end + bias_cols][None],
        attn_share[:shard_rows, q_cols + head_dim :],
        small_share[q_bias_end + bias_cols : q_bias_end + 2 * bias_cols][None],
        o_share,
        small_share[shard_rows : 2 * shard_rows],
        gate_share,
        up_share,
        down_share,
    )


def solution(mesh):
    placed = (
        P("fsdp", "ctx", None),
        P("fsdp", "ctx"),
        P("fsdp"),
        P("fsdp", "tp"),
        P("tp", "fsdp"),
        P("fsdp", "tp"),
        P("tp", "fsdp"),
        P("fsdp", "tp"),
        P("tp", "fsdp"),
        P("tp", "fsdp"),
        P("fsdp"),
        P("fsdp", "tp"),
        P("fsdp", "tp"),
        P("tp", "fsdp"),
        P("fsdp", "ctx", None),
    )
    return jax.shard_map(
        body,
        mesh=mesh,
        in_specs=placed,
        out_specs=(
            P("fsdp", "ctx", None),
            P("fsdp", "ctx", None),
            P("fsdp"),
            P("fsdp", "tp"),
            P("tp", "fsdp"),
            P("fsdp", "tp"),
            P("tp", "fsdp"),
            P("fsdp", "tp"),
            P("tp", "fsdp"),
            P("tp", "fsdp"),
            P("fsdp"),
            P("fsdp", "tp"),
            P("fsdp", "tp"),
            P("tp", "fsdp"),
        ),
        check_vma=False,
    )
```

time: 1200 us -> 794 us (0.66)
  waiting for transfers between devices: 760 us -> 124 us
  starting transfers between devices: 1.01 us -> 330 us
  blocking collectives: 213 us -> 0 us
  local copies, waits for them, and re-layouts: 49 us -> 135 us
  other arithmetic: 43.8 us -> 98.9 us
  matrix products: 108 us -> 87.8 us
  between operations: 19.4 us -> 4.38 us
    reduce_scatter x5 -> x0, waiting for transfers between devices: 341 us -> none  [the longest x1 92.5 us: body(): lax.psum_scatter(full_grads[10].astype(jnp.bfloat16), 'fsdp', scatter_dim...]
    ppermute x0 -> x151, starting transfers between devices: none -> 330 us  [the longest x15 99.1 us: scatter_sum(): up = lax.ppermute(low(sum_up), 'fsdp', [(i, i + 2) for i in valid_up])]
    all_gather x3 -> x0, waiting for transfers between devices: 192 us -> none  [the longest x1 68.9 us: body(): lax.all_gather(up_weight, 'fsdp', axis=0, tiled=True)]
    all_gather x6 -> x0, blocking collectives: 158 us -> none  [the longest x1 32.4 us: body(): lax.all_gather(q_weight, 'fsdp', axis=0, tiled=True)]
    unnamed x18 -> x0, waiting for transfers between devices: 149 us -> none
    ppermute x0 -> x151, waiting for transfers between devices: none -> 124 us  [the longest x15 39.8 us: gather_pieces(): lax.ppermute(above[-1], 'fsdp', [(i, i - 2) for i in range(2, count) if i...]
    psum x4 -> x0, waiting for transfers between devices: 78.4 us -> none  [the longest x1 22.8 us: body(): lax.psum(product(hidden, w_down).astype(jnp.bfloat16), 'tp')]
    unnamed x2 -> x0, blocking collectives: 45.8 us -> none
  transfers between devices with their start and end apart: 15 -> 151, of which waited for: 14 -> 37; matrix products, arithmetic and copies ran while one was open for 6% -> 38% of each run, Pallas kernels for 0% -> 0%
where the time goes in v1:
time: 794 us; the launch traced here: 780 us
  starting transfers between devices  330 us (42%)
  local copies, waits for them, and re-layouts  135 us (17%)
  waiting for transfers between devices  124 us (16%)
  other arithmetic  98.9 us (12%)
  matrix products  87.8 us (11%)
    ppermute x15, starting transfers between devices, scatter_sum(): up = lax.ppermute(low(sum_up), 'fsdp', [(i, i + 2) for i in valid_up])  99.1 us
    ppermute x35, starting transfers between devices, pair_sum(): lax.ppermute(block(target, 1 - x), 'fsdp', pairs)  63 us
    ppermute x15, starting transfers between devices, gather_pieces(): lax.ppermute(below[-1], 'fsdp', [(i, i + 2) for i in range(count - 2) if...  58 us
    ppermute x15, starting transfers between devices, gather_pieces(): lax.ppermute(above[-1], 'fsdp', [(i, i ^ 1) for i in range(count) if i //...  45.6 us
    ppermute x15, waiting for transfers between devices, gather_pieces(): lax.ppermute(above[-1], 'fsdp', [(i, i - 2) for i in range(2, count) if i...  39.8 us
    dot_general x7, matrix products, inner_prod(): lax.dot_general(left, right, (((0,), (0,)), ((), ())), preferred_element_...  31.5 us
    dot_general x10, matrix products, times_trans(): lax.dot_general(left, right, (((1,), (1,)), ((), ())), preferred_element_...  31.5 us
    convert_element_type x40, other arithmetic, low(): return value.astype(jnp.bfloat16)  31.4 us
  transfers between devices with their start and end apart: 151, of which 37 were waited for; matrix products, arithmetic and copies ran while one was open for 38% of the time, Pallas kernels for 0%

profile of v1, /device:TPU:0, one launch (start us, length us, event | category | flops | bytes accessed | tf_op | source)
XLA Modules:
  0.0 780.1 jit_solution(8901131487216231484)
XLA Ops:
  45.4 10.2 %collective-permute-start.43 = (bf16[112,1216]{1,0:T(8,128)(2,1)}, bf16[112,1216]{1,0:T(8,128)(2,1)}, u32[]{:S(2)}, u32[]{:S(2)}) collective-permute-start(bf16[112,1216]{1,0:T(8,128)(2,1)} %get-tuple-element.97), channel_id=1, source_target_pairs={{0,8},{4,12},{8,16},{12,20},{16,24},{20,28},{1,9},{5,13},{9,17},{1... | collective-permute-start | bytes 817160 | tf_op jit(solution)/shard_map/ppermute | solution.py:70
  59.0 5.9 collective-permute-done.28
  79.2 4.8 collective-permute-done.24
  120.1 5.9 collective-permute-start.30
  133.1 15.1 %collective-permute-start.44 = (bf16[112,1216]{1,0:T(8,128)(2,1)}, bf16[112,1216]{1,0:T(8,128)(2,1)}, u32[]{:S(2)}, u32[]{:S(2)}) collective-permute-start(bf16[112,1216]{1,0:T(8,128)(2,1)} %collective-permute-done.43), channel_id=1, source_target_pairs={{8,16},{12,20},{16,24},{20,28},{9,17},{13,21},{17,25},{21,29},{10,... | collective-permute-start | bytes 817160 | tf_op jit(solution)/shard_map/ppermute | solution.py:70
  192.8 4.6 fusion.40
  201.2 11.1 %collective-permute-start.56 = (bf16[112,1216]{1,0:T(8,128)(2,1)}, bf16[112,1216]{1,0:T(8,128)(2,1)}, u32[]{:S(2)}, u32[]{:S(2)}) collective-permute-start(bf16[112,1216]{1,0:T(8,128)(2,1)} %get-tuple-element.91), channel_id=1, source_target_pairs={{0,8},{4,12},{8,16},{12,20},{16,24},{20,28},{1,9},{5,13},{9,17},{1... | collective-permute-start | bytes 817160 | tf_op jit(solution)/shard_map/ppermute | solution.py:70
  220.4 4.8 fusion
  225.5 5.0 fusion.164
  258.4 6.3 collective-permute-done.49
  266.7 17.6 %collective-permute-done.51 = bf16[112,1216]{1,0:T(8,128)(2,1)S(1)} collective-permute-done((bf16[112,1216]{1,0:T(8,128)(2,1)S(1)}, bf16[112,1216]{1,0:T(8,128)(2,1)S(1)}, u32[]{:S(2)}, u32[]{:S(2)}) %collective-permute-start.51) | collective-permute-done | bytes 272416 | tf_op jit(solution)/shard_map/ppermute | solution.py:75
  299.1 4.5 collective-permute-done.36
  308.1 7.3 collective-permute-done.38
  317.7 7.6 collective-permute-done.64
  331.2 4.4 collective-permute-done.52
  339.3 4.8 collective-permute-done.65
  406.7 5.4 convolution_convert_fusion.2
  427.6 5.4 collective-permute-done.112
  447.1 5.1 collective-permute-done.125
  456.6 5.8 collective-permute-done.111
  490.6 8.4 %collective-permute-done.71 = bf16[256,896]{1,0:T(8,128)(2,1)S(1)} collective-permute-done((bf16[256,896]{1,0:T(8,128)(2,1)S(1)}, bf16[256,896]{1,0:T(8,128)(2,1)S(1)}, u32[]{:S(2)}, u32[]{:S(2)}) %collective-permute-start.71) | collective-permute-done | bytes 458784 | tf_op jit(solution)/shard_map/ppermute | solution.py:158
  510.9 8.6 %collective-permute-start.143 = (bf16[112,1216]{1,0:T(8,128)(2,1)}, bf16[112,1216]{1,0:T(8,128)(2,1)}, u32[]{:S(2)}, u32[]{:S(2)}) collective-permute-start(bf16[112,1216]{1,0:T(8,128)(2,1)} %get-tuple-element.111), channel_id=1, source_target_pairs={{0,8},{4,12},{8,16},{12,20},{16,24},{20,28},{1,9},{5,13},{9,17},{1... | collective-permute-start | bytes 817160 | tf_op jit(solution)/shard_map/ppermute | solution.py:138
  538.3 9.9 %multiply_convert_fusion = bf16[3584,1024]{0,1:T(8,128)(2,1)S(1)} fusion(f32[3584,1024]{0,1:T(8,128)} %copy-done.6, bf16[3584,64]{1,0:T(8,128)(2,1)} %reshape.372, f32[3584]{0:T(1024)S(1)} %multiply_reduce_fusion.1, f32[3584]{0:T(1024)S(1)} %copy-done.91, bf16[1024,128]{0,1:T(8,128)(2,1)S(1)} %copy-done.50, s32[3584]{0:T(1024)S(1)} %copy-done.78, ...), kind=kOutput, calls=%fused_computation | convolution fusion | flops 506462208 | bytes 22679552 | tf_op jit(solution)/shard_map/dot_general | solution.py:22
  559.8 6.3 convolution_convert_fusion.10
  566.2 7.9 %fusion.48 = bf16[1024,64]{0,1:T(8,128)(2,1)} fusion(bf16[3584,64]{1,0:T(8,128)(2,1)S(1)} %copy-done.9, f32[3584,1024]{0,1:T(8,128)} %copy-done.6, f32[3584]{0:T(1024)S(1)} %copy-done.92, s32[3584]{0:T(1024)S(1)} %copy-done.79, s32[3584]{0:T(1024)S(1)} %copy-done.82, s32[1024]{0:T(1024)S(1)} %copy-done.95), kind=kOutput, calls=%fused_computation.87 | convolution fusion | flops 495517696 | bytes 15316992 | tf_op jit(solution)/shard_map/dot_general | solution.py:16
  599.7 35.7 %collective-permute-start.99 = (bf16[112,448]{1,0:T(8,128)(2,1)}, bf16[112,448]{1,0:T(8,128)(2,1)}, u32[]{:S(2)}, u32[]{:S(2)}) collective-permute-start(bf16[112,448]{1,0:T(8,128)(2,1)} %fusion.118), channel_id=1, source_target_pairs={{0,8},{4,12},{1,9},{5,13},{2,10},{6,14},{3,11},{7,15}} | collective-permute-start | bytes 301064 | tf_op jit(solution)/shard_map/ppermute | solution.py:138
  661.6 4.6 collective-permute-start.100
  691.4 11.7 %collective-permute-start.101 = (bf16[112,448]{1,0:T(8,128)(2,1)S(1)}, bf16[112,448]{1,0:T(8,128)(2,1)S(1)}, u32[]{:S(2)}, u32[]{:S(2)}) collective-permute-start(bf16[112,448]{1,0:T(8,128)(2,1)S(1)} %get-tuple-element.156), channel_id=1, source_target_pairs={{0,8},{4,12},{8,16},{12,20},{16,24},{20,28},{1,9},{5,13},{9,17},{1... | collective-permute-start | bytes 301064 | tf_op jit(solution)/shard_map/ppermute | solution.py:138
  715.4 5.2 constant_dynamic-slice_fusion.12
  742.0 6.1 collective-permute-start.85
  758.8 4.4 collective-permute-start.87
  765.9 4.5 collective-permute-done.93
  (747 shorter events, 520.8 us)
Async XLA Ops:
  8.9 32.3 %collective-permute-start = (bf16[128,576]{1,0:T(8,128)(2,1)}, bf16[128,576]{1,0:T(8,128)(2,1)}, u32[]{:S(2)}, u32[]{:S(2)}) collective-permute-start(bf16[128,576]{1,0:T(8,128)(2,1)} %pad_maximum_fusion.10), channel_id=1, source_target_pairs={{0,4},{4,0},{8,12},{12,8},{16,20},{20,16},{24,28},{28,24},{1,5},{5... | collective-permute-start | bytes 442376 | tf_op jit(solution)/shard_map/ppermute | solution.py:66
  11.8 75.2 %collective-permute-start.2 = (bf16[128,576]{1,0:T(8,128)(2,1)}, bf16[128,576]{1,0:T(8,128)(2,1)}, u32[]{:S(2)}, u32[]{:S(2)}) collective-permute-start(bf16[128,576]{1,0:T(8,128)(2,1)} %pad_maximum_fusion.10), channel_id=1, source_target_pairs={{0,8},{4,12},{8,16},{12,20},{16,24},{20,28},{1,9},{5,13},{9,17},{1... | collective-permute-start | bytes 442376 | tf_op jit(solution)/shard_map/ppermute | solution.py:70
  36.1 65.1 %collective-permute-start.1 = (bf16[128,576]{1,0:T(8,128)(2,1)}, bf16[128,576]{1,0:T(8,128)(2,1)}, u32[]{:S(2)}, u32[]{:S(2)}) collective-permute-start(bf16[128,576]{1,0:T(8,128)(2,1)} %pad_maximum_fusion.10), channel_id=1, source_target_pairs={{8,0},{12,4},{16,8},{20,12},{24,16},{28,20},{9,1},{13,5},{17,9},{2... | collective-permute-start | bytes 442376 | tf_op jit(solution)/shard_map/ppermute | solution.py:75
  45.4 86.4 %collective-permute-start.43 = (bf16[112,1216]{1,0:T(8,128)(2,1)}, bf16[112,1216]{1,0:T(8,128)(2,1)}, u32[]{:S(2)}, u32[]{:S(2)}) collective-permute-start(bf16[112,1216]{1,0:T(8,128)(2,1)} %get-tuple-element.97), channel_id=1, source_target_pairs={{0,8},{4,12},{8,16},{12,20},{16,24},{20,28},{1,9},{5,13},{9,17},{1... | collective-permute-start | bytes 817160 | tf_op jit(solution)/shard_map/ppermute | solution.py:70
  101.2 131.7 %collective-permute-start.42 = (bf16[112,1216]{1,0:T(8,128)(2,1)}, bf16[112,1216]{1,0:T(8,128)(2,1)}, u32[]{:S(2)}, u32[]{:S(2)}) collective-permute-start(bf16[112,1216]{1,0:T(8,128)(2,1)} %get-tuple-element.97), channel_id=1, source_target_pairs={{8,0},{12,4},{16,8},{20,12},{24,16},{28,20},{9,1},{13,5},{17,9},{2... | collective-permute-start | bytes 817160 | tf_op jit(solution)/shard_map/ppermute | solution.py:75
  120.1 81.0 %collective-permute-start.30 = (bf16[112,1216]{1,0:T(8,128)(2,1)}, bf16[112,1216]{1,0:T(8,128)(2,1)}, u32[]{:S(2)}, u32[]{:S(2)}) collective-permute-start(bf16[112,1216]{1,0:T(8,128)(2,1)} %get-tuple-element.93), channel_id=1, source_target_pairs={{0,8},{4,12},{8,16},{12,20},{16,24},{20,28},{1,9},{5,13},{9,17},{1... | collective-permute-start | bytes 817160 | tf_op jit(solution)/shard_map/ppermute | solution.py:70
  131.8 106.2 %collective-permute-start.29 = (bf16[112,1216]{1,0:T(8,128)(2,1)}, bf16[112,1216]{1,0:T(8,128)(2,1)}, u32[]{:S(2)}, u32[]{:S(2)}) collective-permute-start(bf16[112,1216]{1,0:T(8,128)(2,1)} %get-tuple-element.93), channel_id=1, source_target_pairs={{8,0},{12,4},{16,8},{20,12},{24,16},{28,20},{9,1},{13,5},{17,9},{2... | collective-permute-start | bytes 817160 | tf_op jit(solution)/shard_map/ppermute | solution.py:75
  133.1 79.2 %collective-permute-start.44 = (bf16[112,1216]{1,0:T(8,128)(2,1)}, bf16[112,1216]{1,0:T(8,128)(2,1)}, u32[]{:S(2)}, u32[]{:S(2)}) collective-permute-start(bf16[112,1216]{1,0:T(8,128)(2,1)} %collective-permute-done.43), channel_id=1, source_target_pairs={{8,16},{12,20},{16,24},{20,28},{9,17},{13,21},{17,25},{21,29},{10,... | collective-permute-start | bytes 817160 | tf_op jit(solution)/shard_map/ppermute | solution.py:70
  160.4 53.3 %collective-permute-start.13 = (bf16[512,128]{0,1:T(8,128)(2,1)}, bf16[512,128]{0,1:T(8,128)(2,1)}, u32[]{:S(2)}, u32[]{:S(2)}) collective-permute-start(bf16[512,128]{0,1:T(8,128)(2,1)} %pad_maximum_fusion.13), channel_id=1, source_target_pairs={{2,0},{0,2},{3,1},{1,3},{6,4},{4,6},{7,5},{5,7},{10,8},{8,10},{11,... | collective-permute-start | bytes 393224 | tf_op jit(solution)/shard_map/ppermute | solution.py:153
  201.2 33.1 %collective-permute-start.56 = (bf16[112,1216]{1,0:T(8,128)(2,1)}, bf16[112,1216]{1,0:T(8,128)(2,1)}, u32[]{:S(2)}, u32[]{:S(2)}) collective-permute-start(bf16[112,1216]{1,0:T(8,128)(2,1)} %get-tuple-element.91), channel_id=1, source_target_pairs={{0,8},{4,12},{8,16},{12,20},{16,24},{20,28},{1,9},{5,13},{9,17},{1... | collective-permute-start | bytes 817160 | tf_op jit(solution)/shard_map/ppermute | solution.py:70
  212.3 22.6 %collective-permute-start.31 = (bf16[112,1216]{1,0:T(8,128)(2,1)}, bf16[112,1216]{1,0:T(8,128)(2,1)}, u32[]{:S(2)}, u32[]{:S(2)}) collective-permute-start(bf16[112,1216]{1,0:T(8,128)(2,1)} %collective-permute-done.30), channel_id=1, source_target_pairs={{8,16},{12,20},{16,24},{20,28},{9,17},{13,21},{17,25},{21,29},{10,... | collective-permute-start | bytes 817160 | tf_op jit(solution)/shard_map/ppermute | solution.py:70
  244.8 83.6 %collective-permute-start.53 = (bf16[112,1216]{1,0:T(8,128)(2,1)}, bf16[112,1216]{1,0:T(8,128)(2,1)S(1)}, u32[]{:S(2)}, u32[]{:S(2)}) collective-permute-start(bf16[112,1216]{1,0:T(8,128)(2,1)} %collective-permute-done.43), channel_id=1, source_target_pairs={{8,12},{12,8},{16,20},{20,16},{24,28},{28,24},{9,13},{13,9},{17,21... | collective-permute-start | bytes 817160 | tf_op jit(solution)/shard_map/ppermute | solution.py:82
  247.4 37.6 %collective-permute-start.33 = (bf16[112,1216]{1,0:T(8,128)(2,1)}, bf16[112,1216]{1,0:T(8,128)(2,1)S(1)}, u32[]{:S(2)}, u32[]{:S(2)}) collective-permute-start(bf16[112,1216]{1,0:T(8,128)(2,1)} %collective-permute-done.29), channel_id=1, source_target_pairs={{0,4},{4,0},{8,12},{12,8},{16,20},{20,16},{1,5},{5,1},{9,13},{13,9... | collective-permute-start | bytes 817160 | tf_op jit(solution)/shard_map/ppermute | solution.py:87
  250.4 39.3 %collective-permute-start.35 = (bf16[112,1216]{1,0:T(8,128)(2,1)}, bf16[112,1216]{1,0:T(8,128)(2,1)S(1)}, u32[]{:S(2)}, u32[]{:S(2)}) collective-permute-start(bf16[112,1216]{1,0:T(8,128)(2,1)} %collective-permute-done.29), channel_id=1, source_target_pairs={{8,0},{12,4},{16,8},{20,12},{9,1},{13,5},{17,9},{21,13},{10,2},{14... | collective-permute-start | bytes 817160 | tf_op jit(solution)/shard_map/ppermute | solution.py:75
  264.6 82.7 %collective-permute-start.40 = (bf16[112,1216]{1,0:T(8,128)(2,1)}, bf16[112,1216]{1,0:T(8,128)(2,1)S(1)}, u32[]{:S(2)}, u32[]{:S(2)}) collective-permute-start(bf16[112,1216]{1,0:T(8,128)(2,1)} %collective-permute-done.30), channel_id=1, source_target_pairs={{8,12},{12,8},{16,20},{20,16},{24,28},{28,24},{9,13},{13,9},{17,21... | collective-permute-start | bytes 817160 | tf_op jit(solution)/shard_map/ppermute | solution.py:82
  294.3 45.0 %collective-permute-start.66 = (bf16[112,1216]{1,0:T(8,128)(2,1)}, bf16[112,1216]{1,0:T(8,128)(2,1)S(1)}, u32[]{:S(2)}, u32[]{:S(2)}) collective-permute-start(bf16[112,1216]{1,0:T(8,128)(2,1)} %collective-permute-done.56), channel_id=1, source_target_pairs={{8,12},{12,8},{16,20},{20,16},{24,28},{28,24},{9,13},{13,9},{17,21... | collective-permute-start | bytes 817160 | tf_op jit(solution)/shard_map/ppermute | solution.py:82
  317.5 29.9 %collective-permute-start.27 = (bf16[512,896]{1,0:T(8,128)(2,1)S(1)}, bf16[512,896]{1,0:T(8,128)(2,1)S(1)}, u32[]{:S(2)}, u32[]{:S(2)}) collective-permute-start(bf16[512,896]{1,0:T(8,128)(2,1)S(1)} %convolution_convert_fusion.7), channel_id=1, source_target_pairs={{0,1},{1,0},{2,3},{3,2},{4,5},{5,4},{6,7},{7,6},{8,9},{9,8},{10,11... | collective-permute-start | bytes 2752520 | tf_op jit(solution)/shard_map/ppermute | solution.py:148
  357.9 131.9 %collective-permute-start.67 = (bf16[256,896]{1,0:T(8,128)(2,1)}, bf16[256,896]{1,0:T(8,128)(2,1)}, u32[]{:S(2)}, u32[]{:S(2)}) collective-permute-start(bf16[256,896]{1,0:T(8,128)(2,1)} %constant_dynamic-slice_fusion.17), channel_id=1, source_target_pairs={{0,1},{1,0},{2,3},{3,2},{4,5},{5,4},{6,7},{7,6},{8,9},{9,8},{10,11... | collective-permute-start | bytes 1376264 | tf_op jit(solution)/shard_map/ppermute | solution.py:148
  363.6 137.3 %collective-permute-start.73 = (bf16[256,896]{1,0:T(8,128)(2,1)}, bf16[256,896]{1,0:T(8,128)(2,1)}, u32[]{:S(2)}, u32[]{:S(2)}) collective-permute-start(bf16[256,896]{1,0:T(8,128)(2,1)} %constant_dynamic-slice_fusion.14), channel_id=1, source_target_pairs={{0,1},{1,0},{2,3},{3,2},{4,5},{5,4},{6,7},{7,6},{8,9},{9,8},{10,11... | collective-permute-start | bytes 1376264 | tf_op jit(solution)/shard_map/ppermute | solution.py:148
  390.1 32.5 %collective-permute-start.140 = (bf16[112,1216]{1,0:T(8,128)(2,1)}, bf16[112,1216]{1,0:T(8,128)(2,1)}, u32[]{:S(2)}, u32[]{:S(2)}) collective-permute-start(bf16[112,1216]{1,0:T(8,128)(2,1)} %get-tuple-element.108), channel_id=1, source_target_pairs={{0,4},{4,0},{1,5},{5,1},{2,6},{6,2},{3,7},{7,3}} | collective-permute-start | bytes 817160 | tf_op jit(solution)/shard_map/ppermute | solution.py:127
  393.4 44.2 %collective-permute-start.139 = (bf16[112,1216]{1,0:T(8,128)(2,1)}, bf16[112,1216]{1,0:T(8,128)(2,1)}, u32[]{:S(2)}, u32[]{:S(2)}) collective-permute-start(bf16[112,1216]{1,0:T(8,128)(2,1)} %get-tuple-element.109), channel_id=1, source_target_pairs={{0,4},{4,0},{8,12},{12,8},{1,5},{5,1},{9,13},{13,9},{2,6},{6,2},{1... | collective-permute-start | bytes 817160 | tf_op jit(solution)/shard_map/ppermute | solution.py:127
  403.1 23.4 %collective-permute-start.126 = (bf16[112,1216]{1,0:T(8,128)(2,1)}, bf16[112,1216]{1,0:T(8,128)(2,1)}, u32[]{:S(2)}, u32[]{:S(2)}) collective-permute-start(bf16[112,1216]{1,0:T(8,128)(2,1)} %get-tuple-element.117), channel_id=1, source_target_pairs={{0,4},{4,0},{1,5},{5,1},{2,6},{6,2},{3,7},{7,3}} | collective-permute-start | bytes 817160 | tf_op jit(solution)/shard_map/ppermute | solution.py:127
  434.8 31.5 %collective-permute-start.138 = (bf16[112,1216]{1,0:T(8,128)(2,1)S(1)}, bf16[112,1216]{1,0:T(8,128)(2,1)S(1)}, u32[]{:S(2)}, u32[]{:S(2)}) collective-permute-start(bf16[112,1216]{1,0:T(8,128)(2,1)S(1)} %copy-done.68), channel_id=1, source_target_pairs={{0,4},{4,0},{8,12},{12,8},{16,20},{20,16},{1,5},{5,1},{9,13},{13,9... | collective-permute-start | bytes 817160 | tf_op jit(solution)/shard_map/ppermute | solution.py:127
  500.9 155.3 %collective-permute-start.137 = (bf16[112,1216]{1,0:T(8,128)(2,1)}, bf16[112,1216]{1,0:T(8,128)(2,1)}, u32[]{:S(2)}, u32[]{:S(2)}) collective-permute-start(bf16[112,1216]{1,0:T(8,128)(2,1)} %get-tuple-element.104), channel_id=1, source_target_pairs={{0,4},{4,0},{8,12},{12,8},{16,20},{20,16},{24,28},{28,24},{1,5},{5... | collective-permute-start | bytes 817160 | tf_op jit(solution)/shard_map/ppermute | solution.py:127
  510.9 146.6 %collective-permute-start.143 = (bf16[112,1216]{1,0:T(8,128)(2,1)}, bf16[112,1216]{1,0:T(8,128)(2,1)}, u32[]{:S(2)}, u32[]{:S(2)}) collective-permute-start(bf16[112,1216]{1,0:T(8,128)(2,1)} %get-tuple-element.111), channel_id=1, source_target_pairs={{0,8},{4,12},{8,16},{12,20},{16,24},{20,28},{1,9},{5,13},{9,17},{1... | collective-permute-start | bytes 817160 | tf_op jit(solution)/shard_map/ppermute | solution.py:138
  523.0 138.5 %collective-permute-start.149 = (bf16[112,1216]{1,0:T(8,128)(2,1)}, bf16[112,1216]{1,0:T(8,128)(2,1)}, u32[]{:S(2)}, u32[]{:S(2)}) collective-permute-start(bf16[112,1216]{1,0:T(8,128)(2,1)} %fusion.62), channel_id=1, source_target_pairs={{8,0},{12,4},{16,8},{20,12},{24,16},{28,20},{9,1},{13,5},{17,9},{2... | collective-permute-start | bytes 817160 | tf_op jit(solution)/shard_map/ppermute | solution.py:139
  581.5 71.6 %collective-permute-start.97 = (bf16[112,448]{1,0:T(8,128)(2,1)}, bf16[112,448]{1,0:T(8,128)(2,1)}, u32[]{:S(2)}, u32[]{:S(2)}) collective-permute-start(bf16[112,448]{1,0:T(8,128)(2,1)} %get-tuple-element.154), channel_id=1, source_target_pairs={{0,4},{4,0},{8,12},{12,8},{1,5},{5,1},{9,13},{13,9},{2,6},{6,2},{1... | collective-permute-start | bytes 301064 | tf_op jit(solution)/shard_map/ppermute | solution.py:127
  599.7 54.7 %collective-permute-start.99 = (bf16[112,448]{1,0:T(8,128)(2,1)}, bf16[112,448]{1,0:T(8,128)(2,1)}, u32[]{:S(2)}, u32[]{:S(2)}) collective-permute-start(bf16[112,448]{1,0:T(8,128)(2,1)} %fusion.118), channel_id=1, source_target_pairs={{0,8},{4,12},{1,9},{5,13},{2,10},{6,14},{3,11},{7,15}} | collective-permute-start | bytes 301064 | tf_op jit(solution)/shard_map/ppermute | solution.py:138
  679.3 28.6 %collective-permute-start.95 = (bf16[112,448]{1,0:T(8,128)(2,1)S(1)}, bf16[112,448]{1,0:T(8,128)(2,1)S(1)}, u32[]{:S(2)}, u32[]{:S(2)}) collective-permute-start(bf16[112,448]{1,0:T(8,128)(2,1)S(1)} %copy-done.72), channel_id=1, source_target_pairs={{0,4},{4,0},{8,12},{12,8},{16,20},{20,16},{24,28},{28,24},{1,5},{5... | collective-permute-start | bytes 301064 | tf_op jit(solution)/shard_map/ppermute | solution.py:127
  681.6 30.4 %collective-permute-start.80 = (bf16[512,896]{1,0:T(8,128)(2,1)S(1)}, bf16[512,896]{1,0:T(8,128)(2,1)S(1)}, u32[]{:S(2)}, u32[]{:S(2)}) collective-permute-start(bf16[512,896]{1,0:T(8,128)(2,1)S(1)} %copy-done.10), channel_id=1, source_target_pairs={{0,1},{1,0},{2,3},{3,2},{4,5},{5,4},{6,7},{7,6},{8,9},{9,8},{10,11... | collective-permute-start | bytes 2752520 | tf_op jit(solution)/shard_map/ppermute | solution.py:148
  732.6 24.1 %collective-permute-start.82 = (bf16[128,576]{0,1:T(8,128)(2,1)S(1)}, bf16[128,576]{0,1:T(8,128)(2,1)S(1)}, u32[]{:S(2)}, u32[]{:S(2)}) collective-permute-start(bf16[128,576]{0,1:T(8,128)(2,1)S(1)} %bitcast.307), channel_id=1, source_target_pairs={{0,4},{4,0},{8,12},{12,8},{16,20},{20,16},{1,5},{5,1},{9,13},{13,9... | collective-permute-start | bytes 442376 | tf_op jit(solution)/shard_map/ppermute | solution.py:127
  740.3 22.9 %collective-permute-start.88 = (bf16[128,576]{0,1:T(8,128)(2,1)S(1)}, bf16[128,576]{0,1:T(8,128)(2,1)S(1)}, u32[]{:S(2)}, u32[]{:S(2)}) collective-permute-start(bf16[128,576]{0,1:T(8,128)(2,1)S(1)} %bitcast.308), channel_id=1, source_target_pairs={{8,12},{12,8},{16,20},{20,16},{24,28},{28,24},{9,13},{13,9},{17,21... | collective-permute-start | bytes 442376 | tf_op jit(solution)/shard_map/ppermute | solution.py:127
  (224 other events, 2776.8 us)
